TPU v7x, 32 devices: a whole 2x2x4 slice. The times are simulated.
32 devices in a mesh: grp: 4 (over y, x), blk: 8 (over z, core).
Axes of the slice: x: 2, y: 2, z: 4, core: 2. Of those that a mesh axis runs over, the one named last changes fastest.
Arguments:
- raw_blocks: bfloat16 [16, 24, 64, 256], P('blk', 'grp'), may hold values from -1.5 to 1.5
- metric_factor: bfloat16 [256, 256], replicated, may hold values from -0.375 to 0.375
- sig_list: int32 [16, 24], P('blk', 'grp'), may hold values from 0 to 15, as said below
- live_count: int32 [16, 4], P('blk', 'grp'), may hold values from 1 to 6, as said below
Outputs:
- exchange: float32 [1024, 1024], P('blk', 'grp')
Inputs may be any that keep to these rules, and one draw needn't show every extreme that they name: `sig_list`: the 6 slots of one row block in one group name distinct orbital blocks. `live_count`: for every group, each aligned run of 2 row blocks holds a row block with all 6 slots live.
All inputs are finite; a program needn't handle non-finite values.
Results may differ from a plain program's by a relative error of at most 0.0011.
Values may be sent and summed in bfloat16 or wider, within the bound.
A program may use at most 64 MiB of HBM per device.

v0:
```python
import jax
import jax.numpy as jnp
from jax import lax
from jax.sharding import PartitionSpec as P

NOB_DEV = 16


def contract(raw_blocks, metric_factor, live_count):
    product = jnp.einsum(
        "msua,ab->msub", raw_blocks, metric_factor, preferred_element_type=jnp.float32
    )
    live_mask = jnp.arange(raw_blocks.shape[1], dtype=jnp.int32)[None, :] < live_count
    return (product * live_mask[:, :, None, None].astype(jnp.float32)).astype(jnp.bfloat16)


def dense_rows(contracted, sig_list):
    one_hot = (sig_list[:, :, None] == jnp.arange(NOB_DEV, dtype=jnp.int32)[None, None, :]).astype(
        jnp.bfloat16
    )
    return jnp.einsum(
        "msn,msua->mnua", one_hot, contracted, preferred_element_type=jnp.float32
    ).astype(jnp.bfloat16)


def pair_blocks(dense, other_x, other_ids):
    chosen = jnp.take(dense, other_ids, axis=1)
    blocks = jnp.einsum("mlsua,lsva->mulv", chosen, other_x, preferred_element_type=jnp.float32)
    return blocks.reshape(dense.shape[0] * dense.shape[2], other_x.shape[0] * other_x.shape[2])


def shards(raw_blocks, metric_factor, sig_list, live_count):
    contracted = contract(raw_blocks, metric_factor, live_count)
    dense = dense_rows(contracted, sig_list)
    row_blocks = raw_blocks.shape[0]
    width = raw_blocks.shape[2]
    rows_here = row_blocks * width
    cycle_size = lax.axis_size("blk")
    strip = jnp.zeros((rows_here, cycle_size * rows_here), jnp.float32)
    piece_x = lax.all_gather(contracted, "blk", axis=0, tiled=True)
    piece_ids = lax.all_gather(sig_list, "blk", axis=0, tiled=True)
    piece_rows = piece_x.shape[0]
    step_rows = max([divisor for divisor in range(1, 17) if piece_rows % divisor == 0])

    def one_turn(turn_index, current):
        block_x = lax.dynamic_slice_in_dim(piece_x, turn_index * step_rows, step_rows, 0)
        block_ids = lax.dynamic_slice_in_dim(piece_ids, turn_index * step_rows, step_rows, 0)
        values = pair_blocks(dense, block_x, block_ids)
        return lax.dynamic_update_slice(current, values, (0, turn_index * step_rows * width))

    strip = lax.fori_loop(0, piece_rows // step_rows, one_turn, strip)
    summed = lax.psum_scatter(strip, "grp", scatter_dimension=1, tiled=True)
    return 0.25 * summed


def solution(mesh):
    placed = (P("blk", "grp", None, None), P(), P("blk", "grp"), P("blk", "grp"))
    return jax.shard_map(
        shards, mesh=mesh, in_specs=placed, out_specs=P("blk", "grp"), check_vma=False
    )
```

profile of v0, /device:TPU:0, one launch (start us, length us, event | category | flops | bytes accessed | tf_op | source)
XLA Modules:
  0.0 91.4 jit_solution(2411893557653831065)
XLA Ops:
  6.5 0.0 copy-start
  6.5 0.0 all-gather.3.cloned.1.call-start
  6.5 0.8 compare_convert_fusion
  7.3 0.2 copy-done
  7.5 1.9 %fusion.11 = bf16[2,6,64,256]{3,2,1,0:T(8,128)(2,1)} fusion(bf16[2,6,64,256]{3,2,1,0:T(8,128)(2,1)S(1)} %copy-done, f32[2,6]{1,0:T(2,128)S(1)} %compare_convert_fusion, bf16[256,256]{1,0:T(8,128)(2,1)} %param.5), kind=kOutput, calls=%fused_computation.10 | convolution fusion | flops 101056512 | bytes 917552 | tf_op jit(solution)/shard_map/msua,ab->msub/dot_general | solution.py:10
  9.5 0.0 all-gather.3.cloned.1.call-update
  9.5 0.0 reduce-scatter.2.cloned.1.call-start
  9.5 1.7 %convolution_convert_fusion = bf16[2,16,64,256]{3,1,2,0:T(8,128)(2,1)S(1)} fusion(bf16[2,6,64,256]{3,2,1,0:T(8,128)(2,1)} %fusion.11, s32[2,6]{1,0:T(2,128)} %param.6), kind=kOutput, calls=%fused_computation.7 | convolution fusion | flops 6815936 | bytes 1441840 | tf_op jit(solution)/shard_map/msn,msua->mnua/dot_general | solution.py:21
  11.2 0.3 copy.12
  11.6 13.8 %all-gather = s32[8,2,6]{2,1,0:T(2,128)S(1)} all-gather(s32[1,2,6]{2,1,0:T(2,128)} %bitcast.41), channel_id=1, replica_groups=mesh['grp'=4,'blk'=8] {'blk'}, dimensions={0}, use_global_device_ids=true | all-gather | bytes 432 | tf_op jit(solution)/shard_map/all_gather | solution.py:41
  25.4 0.1 reshape.37
  25.5 6.0 %gather_fusion = bf16[96,2,64,256]{3,2,1,0:T(8,128)(2,1)} fusion(bf16[2,16,64,256]{3,2,1,0:T(8,128)(2,1)S(1)} %copy.12, s32[1024]{0:T(1024)S(1)} %pad_clamp_fusion), kind=kCustom, calls=%fused_computation | custom fusion | bytes 12583296 | tf_op jit(solution)/shard_map/while/body/eval_jaxpr/jit(_take)/gather | solution.py:27
  31.5 19.2 %all-gather.3.cloned.1.call-done = bf16[16,6,64,256]{3,2,1,0:T(8,128)(2,1)} async-done(((bf16[2,6,64,256]{3,2,1,0:T(8,128)(2,1)}), bf16[16,6,64,256]{3,2,1,0:T(8,128)(2,1)}) %all-gather.3.cloned.1.call-update) | async-done | bytes 3145744 | tf_op jit(solution)/shard_map/all_gather | solution.py:40
  50.6 6.9 %fusion.6 = f32[2,64,16,64]{1,3,0,2:T(8,128)S(1)} fusion(bf16[16,6,2,64,256]{4,3,2,1,0:T(8,128)(2,1)} %bitcast.38, pred[16,6]{1,0:T(8,128)(4,1)S(1)} %compare_and_fusion, bf16[16,6,64,256]{3,2,1,0:T(8,128)(2,1)} %all-gather.3.cloned.1.call-done), kind=kOutput, calls=%fused_computation.8 | convolution fusion | flops 405798912 | bytes 9961568 | tf_op jit(solution)/shard_map/while/body/eval_jaxpr/mlsua,lsva->mulv/dot_general | solution.py:28
  57.6 0.5 copy.14
  58.1 1.1 %reshape.34 = f32[128,1024]{1,0:T(8,128)} reshape(f32[2,64,16,64]{3,2,1,0:T(8,128)S(1)} %copy.14) | data formatting | bytes 1048576 | tf_op jit(solution)/shard_map/while/body/eval_jaxpr/reshape | solution.py:29
  59.2 0.0 reduce-scatter.2.cloned.1.call-update
  59.2 23.8 %reduce-scatter.2.cloned.1.call-done = f32[128,256]{1,0:T(8,128)} async-done(((f32[128,1024]{1,0:T(8,128)}), f32[128,256]{1,0:T(8,128)}) %reduce-scatter.2.cloned.1.call-update) | async-done | bytes 131088 | tf_op jit(solution)/shard_map/reduce_scatter | solution.py:52
  83.0 1.6 %broadcast_multiply_fusion = f32[128,256]{1,0:T(8,128)} fusion(f32[128,256]{1,0:T(8,128)} %reduce-scatter.2.cloned.1.call-done), kind=kLoop, calls=%fused_computation.13 | loop fusion | flops 32768 | bytes 262144 | tf_op jit(solution)/shard_map/mul | solution.py:53
  (3 shorter events, 0.0 us)
Async XLA Ops:
  6.5 1.0 %copy-start = (bf16[2,6,64,256]{3,2,1,0:T(8,128)(2,1)S(1)}, bf16[2,6,64,256]{3,2,1,0:T(8,128)(2,1)}, u32[]{:S(2)}) copy-start(bf16[2,6,64,256]{3,2,1,0:T(8,128)(2,1)} %param.4) | copy-start | bytes 1179652
  6.5 44.1 %all-gather.3.cloned.1.call-start = ((), (), s32[]{:S(2)}) async-start(), calls=%async_computation.1 | async-start | bytes 3538944 | tf_op jit(solution)/shard_map/all_gather | solution.py:40
  9.5 73.5 %reduce-scatter.2.cloned.1.call-start = ((), (), s32[]{:S(2)}) async-start(), calls=%async_computation.2 | async-start | bytes 655360 | tf_op jit(solution)/shard_map/reduce_scatter | solution.py:52
Sparse Core Ops, SparseCore 0:
  9.6 40.9 all-gather.2
  59.3 23.6 reduce-scatter.1
where the time goes:
time: 91.6 us; the launch traced here: 91.4 us
  waiting for transfers between devices  43 us (47%)
  blocking collectives  13.8 us (15%)
  between operations  13.4 us (15%)
  matrix products  10.5 us (11%)
  local copies, waits for them, and re-layouts  8.28 us (9%)
  other arithmetic  2.36 us (3%)
    reduce_scatter x1, waiting for transfers between devices, shards(): summed = lax.psum_scatter(strip, 'grp', scatter_dimension=1, tiled=True)  23.8 us
    all_gather x1, waiting for transfers between devices, shards(): piece_x = lax.all_gather(contracted, 'blk', axis=0, tiled=True)  19.2 us
    all_gather x1, blocking collectives, shards(): piece_ids = lax.all_gather(sig_list, 'blk', axis=0, tiled=True)  13.8 us
    dot_general x1, matrix products, pair_blocks(): jnp.einsum('mlsua,lsva->mulv', chosen, other_x, preferred_element_type=jn...  6.92 us
    gather x1, local copies, waits for them, and re-layouts, pair_blocks(): chosen = jnp.take(dense, other_ids, axis=1)  6 us
    dot_general x1, matrix products, contract(): jnp.einsum('msua,ab->msub', raw_blocks, metric_factor, preferred_element_...  1.92 us
  transfers between devices with their start and end apart: 2, of which 2 were waited for; matrix products, arithmetic and copies ran while one was open for 9% of the time, Pallas kernels for 0%

commit v1 on v0

v1 whole, which is shorter than its diff:
```python
import functools

import jax
import jax.numpy as jnp
from jax import lax
from jax.experimental import pallas as pl
from jax.experimental.pallas import tpu as pltpu
from jax.sharding import PartitionSpec as P

NOB_DEV = 16
MESH = pl.DeviceIdType.MESH
CUTS = 2
LOW, HIGH = 0, 1


def both(*conditions):
    return functools.reduce(jnp.logical_and, conditions)


def kernel(
    chips, groups, raw_hbm, metric_hbm, sig_hbm, live, out,
    raw, metric, sig_vec, sig_own, xs, own, dense, ids_vec, ids, acc, red, half_sum, swap,
    in_sem, id_send, id_recv, id_local, chain_send, chain_recv, share_send, share_recv,
    red_send, red_recv, swap_send, swap_recv,
):
    row_blocks, slots, width, aux = raw_hbm.shape
    part = aux // 2
    rows = row_blocks * width
    cut_rows = slots * width // CUTS
    blk, grp = lax.axis_index("blk"), lax.axis_index("grp")
    chip, core = lax.div(blk, 2), lax.rem(blk, 2)
    sibling = 1 - core
    last = chips - 1

    def contributes(at, to):
        return jnp.logical_not(
            jnp.logical_or(both(at == 0, to == 1), both(at == last, to == last - 1))
        )

    def up_valid(source):
        return both(source >= 0, contributes(chip, source))

    def down_valid(source):
        return both(source <= last, contributes(chip, source))

    def chain_copy(source, half, m, cut, to_chip):
        piece = xs.at[core, source, half, m, pl.ds(cut * cut_rows, cut_rows)]
        return pltpu.make_async_remote_copy(
            src_ref=piece, dst_ref=piece,
            send_sem=chain_send.at[source, half, m, cut],
            recv_sem=chain_recv.at[source, half, m, cut],
            device_id={"blk": to_chip * 2 + core, "grp": grp}, device_id_type=MESH,
        )

    def share_copy(from_core, source, half, m):
        piece = xs.at[from_core, source, half, m]
        return pltpu.make_async_remote_copy(
            src_ref=piece, dst_ref=piece,
            send_sem=share_send.at[source, half, m], recv_sem=share_recv.at[source, half, m],
            device_id={"blk": chip * 2 + sibling, "grp": grp}, device_id_type=MESH,
        )

    def id_copy(slot, to_blk):
        return pltpu.make_async_remote_copy(
            src_ref=sig_vec, dst_ref=ids_vec.at[slot],
            send_sem=id_send.at[to_blk], recv_sem=id_recv.at[slot],
            device_id={"blk": to_blk, "grp": grp}, device_id_type=MESH,
        )

    def red_copy(slot, to_grp):
        return pltpu.make_async_remote_copy(
            src_ref=acc.at[to_grp], dst_ref=red.at[slot],
            send_sem=red_send.at[to_grp], recv_sem=red_recv.at[slot],
            device_id={"blk": blk, "grp": to_grp}, device_id_type=MESH,
        )

    def swap_copy(to_core, slot):
        return pltpu.make_async_remote_copy(
            src_ref=half_sum.at[to_core], dst_ref=swap.at[slot],
            send_sem=swap_send.at[to_core], recv_sem=swap_recv.at[slot],
            device_id={"blk": grp * 2 + to_core, "grp": chip}, device_id_type=MESH,
        )

    loads = [
        pltpu.make_async_copy(source, target, in_sem.at[index])
        for index, (source, target) in enumerate(
            ((raw_hbm, raw), (metric_hbm, metric), (sig_hbm, sig_vec), (sig_hbm, sig_own))
        )
    ]
    for load in loads:
        load.start()

    barrier = pltpu.get_barrier_semaphore()

    def greet_blk(other, carry):
        @pl.when(other != blk)
        def _():
            pl.semaphore_signal(
                barrier, inc=1, device_id={"blk": other, "grp": grp}, device_id_type=MESH
            )
        return carry

    def greet_grp(other, carry):
        @pl.when(other != grp)
        def _():
            pl.semaphore_signal(
                barrier, inc=1, device_id={"blk": blk, "grp": other}, device_id_type=MESH
            )
        return carry

    lax.fori_loop(0, 2 * chips, greet_blk, 0)
    lax.fori_loop(0, groups, greet_grp, 0)

    @pl.when(chip != grp)
    def _():
        for other in range(2):
            pl.semaphore_signal(
                barrier, inc=1, device_id={"blk": grp * 2 + other, "grp": chip}, device_id_type=MESH
            )

    for load in loads:
        load.wait()

    slot_of_row = lax.broadcasted_iota(jnp.int32, (slots * width, aux), 0) // width
    for m in range(row_blocks):
        product = jnp.dot(
            raw[m].reshape(slots * width, aux), metric[...], preferred_element_type=jnp.float32
        )
        kept = jnp.where(slot_of_row < live[0, m], product, 0.0).astype(jnp.bfloat16)
        for half in range(2):
            piece = kept[:, half * part : (half + 1) * part]
            xs[core, chip, half, m] = piece
            for s in range(slots):
                own[half, m, s] = piece[s * width : (s + 1) * width]
            own[half, m, slots] = jnp.zeros((width, part), jnp.bfloat16)
    ids_vec[blk] = sig_vec[...]

    pl.semaphore_wait(barrier, 2 * chips + groups - 2 + jnp.where(chip != grp, 2, 0))

    def send_ids(other, carry):
        @pl.when(other != blk)
        def _():
            id_copy(blk, other).start()
        return carry

    lax.fori_loop(0, 2 * chips, send_ids, 0)

    own_up = both(chip < last - 1)
    own_down = both(chip > 1)
    for m in range(row_blocks):
        for cut in range(CUTS):
            @pl.when(own_up)
            def _():
                chain_copy(chip, LOW, m, cut, chip + 1).start()

            @pl.when(own_down)
            def _():
                chain_copy(chip, HIGH, m, cut, chip - 1).start()

    for half in range(2):
        for m in range(row_blocks):
            share_copy(core, chip, half, m).start()

    for m in range(row_blocks):
        for n in range(NOB_DEV):
            at = jnp.int32(slots)
            for s in range(slots):
                at = jnp.where(sig_own[m, s] == n, s, at)
            for half in range(2):
                dense[half, n, m * width : (m + 1) * width, :] = own[half, m, at]

    acc[...] = jnp.zeros_like(acc)

    def wait_ids(other, carry):
        @pl.when(other != blk)
        def _():
            id_copy(other, other).wait_recv()
        return carry

    lax.fori_loop(0, 2 * chips, wait_ids, 0)
    to_scalar = pltpu.make_async_copy(ids_vec, ids, id_local)
    to_scalar.start()
    to_scalar.wait()

    def add_products(from_core, source, half, m):
        block = jnp.concatenate(
            [xs[from_core, source, half, m, s * width : (s + 1) * width, :] for s in range(slots)],
            axis=1,
        )
        chosen = jnp.concatenate(
            [dense[half, ids[source * 2 + from_core, m, s]] for s in range(slots)], axis=1
        )
        here = pl.ds(pl.multiple_of(m * width, width), width)
        acc[source, from_core, here, :] += lax.dot_general(
            block, chosen, (((1,), (1,)), ((), ())), preferred_element_type=jnp.float32
        )

    def send_partial(source):
        @pl.when(source != grp)
        def _():
            red_copy(grp, source).start()

    for half in range(2):
        for m in range(row_blocks):
            add_products(core, chip, half, m)

    for end, first, second, to_chip in ((0, LOW, HIGH, 1), (last, HIGH, LOW, last - 1)):
        @pl.when(chip == end)
        def _():
            for m in range(row_blocks):
                for cut in range(CUTS):
                    chain_copy(chip, first, m, cut, to_chip).wait_send()
                    chain_copy(chip, second, m, cut, to_chip).start()

    def arrive(source, half, m, onward, to_chip):
        for cut in range(CUTS):
            chain_copy(source, half, m, cut, chip).wait_recv()

            if onward is not None:
                @pl.when(onward)
                def _():
                    chain_copy(source, half, m, cut, to_chip).start()

        share_copy(core, source, half, m).start()

    def use(source, half, m):
        add_products(core, source, half, m)
        share_copy(sibling, source, half, m).wait_recv()
        add_products(sibling, source, half, m)

    def routes(step):
        below, above = chip - step, chip + step
        return (
            (up_valid(below), below, LOW, both(chip < last), chip + 1),
            (down_valid(above), above, HIGH, both(chip > 0), chip - 1),
            (both(step == 2, chip == 1), 0, HIGH, None, None),
            (both(step == 2, chip == last - 1), last, LOW, None, None),
        )

    def take_in(turn):
        step, m = lax.div(turn, row_blocks) + 1, lax.rem(turn, row_blocks)
        for valid, source, half, onward, to_chip in routes(step):
            @pl.when(valid)
            def _():
                arrive(source, half, m, onward, to_chip)

    def multiply(turn):
        step, m = lax.div(turn, row_blocks) + 1, lax.rem(turn, row_blocks)
        for index, (valid, source, half, onward, to_chip) in enumerate(routes(step)):
            @pl.when(valid)
            def _():
                use(source, half, m)

            whole = both(valid, m == row_blocks - 1)
            if index < 2:
                from_end = both(step == 1, source == (0, last)[index])
                whole = both(whole, jnp.logical_not(from_end))

            @pl.when(whole)
            def _():
                send_partial(source)

    def one_turn(turn, carry):
        @pl.when(turn < (chips - 1) * row_blocks)
        def _():
            take_in(turn)

        @pl.when(turn == 0)
        def _():
            for half in range(2):
                for m in range(row_blocks):
                    share_copy(sibling, chip, half, m).wait_recv()
                    add_products(sibling, chip, half, m)
            send_partial(chip)

        @pl.when(turn > 0)
        def _():
            multiply(turn - 1)

        return carry

    lax.fori_loop(0, (chips - 1) * row_blocks + 1, one_turn, 0)

    mine = contributes(chip, grp)
    theirs = both(chip != grp, contributes(grp, chip))

    @pl.when(mine)
    def _():
        for core_at in range(2):
            half_sum[core_at] = acc[grp, core_at]

        def add_group(other, carry):
            @pl.when(other != grp)
            def _():
                red_copy(other, grp).wait_recv()
                for core_at in range(2):
                    half_sum[core_at] += red[other, core_at]
            return carry

        lax.fori_loop(0, groups, add_group, 0)

        @pl.when(chip != grp)
        def _():
            for core_at in range(2):
                swap_copy(core_at, core).start()

        for core_at in range(2):
            out[:, core_at * rows : (core_at + 1) * rows] = 0.25 * half_sum[core_at].T

    @pl.when(theirs)
    def _():
        for core_at in range(2):
            swap_copy(core_at, core_at).wait_recv()

    @pl.when(both(mine, theirs))
    def _():
        for core_at in range(2):
            out[:, core_at * rows : (core_at + 1) * rows] += 0.25 * swap[core_at]

    @pl.when(jnp.logical_not(mine))
    def _():
        for core_at in range(2):
            out[:, core_at * rows : (core_at + 1) * rows] = 0.25 * swap[core_at]

    def done_ids(other, carry):
        @pl.when(other != blk)
        def _():
            id_copy(blk, other).wait_send()
        return carry

    lax.fori_loop(0, 2 * chips, done_ids, 0)

    def done_source(source, carry):
        low_here = jnp.logical_or(
            source == chip,
            jnp.logical_or(
                both(source < chip, contributes(chip, source)),
                both(source == last, chip == last - 1),
            ),
        )
        high_here = jnp.logical_or(
            source == chip,
            jnp.logical_or(
                both(source > chip, contributes(chip, source)),
                both(source == 0, chip == 1),
            ),
        )
        low_sent = jnp.logical_or(
            jnp.where(source == chip, both(own_up, chip > 0), both(source < chip, chip < last)),
            both(source == chip, chip == last),
        )
        high_sent = jnp.logical_or(
            jnp.where(source == chip, both(own_down, chip < last), both(source > chip, chip > 0)),
            both(source == chip, chip == 0),
        )
        for half, here, sent in ((LOW, low_here, low_sent), (HIGH, high_here, high_sent)):
            @pl.when(here)
            def _():
                for m in range(row_blocks):
                    share_copy(core, source, half, m).wait_send()

            @pl.when(sent)
            def _():
                for m in range(row_blocks):
                    for cut in range(CUTS):
                        chain_copy(source, half, m, cut, chip).wait_send()

        @pl.when(both(source != grp, contributes(chip, source)))
        def _():
            red_copy(grp, source).wait_send()

        return carry

    lax.fori_loop(0, chips, done_source, 0)

    @pl.when(both(mine, chip != grp))
    def _():
        for core_at in range(2):
            swap_copy(core_at, core).wait_send()


def exchange_kernel(raw_blocks, metric_factor, sig_list, live_count):
    row_blocks, slots, width, aux = raw_blocks.shape
    blks, groups = lax.axis_size("blk"), lax.axis_size("grp")
    chips = blks // 2
    rows, part = row_blocks * width, aux // 2
    vmem = pl.BlockSpec(memory_space=pltpu.VMEM)
    hbm = pl.BlockSpec(memory_space=pltpu.HBM)
    smem = pl.BlockSpec(memory_space=pltpu.SMEM)
    dma = pltpu.SemaphoreType.DMA
    return pl.pallas_call(
        functools.partial(kernel, chips, groups),
        out_shape=jax.ShapeDtypeStruct((rows, 2 * rows), jnp.float32),
        in_specs=[hbm, hbm, hbm, smem],
        out_specs=vmem,
        scratch_shapes=[
            pltpu.VMEM(raw_blocks.shape, jnp.bfloat16),
            pltpu.VMEM(metric_factor.shape, jnp.bfloat16),
            pltpu.VMEM(sig_list.shape, jnp.int32),
            pltpu.SMEM(sig_list.shape, jnp.int32),
            pltpu.VMEM((2, chips, 2, row_blocks, slots * width, part), jnp.bfloat16),
            pltpu.VMEM((2, row_blocks, slots + 1, width, part), jnp.bfloat16),
            pltpu.VMEM((2, NOB_DEV, rows, part), jnp.bfloat16),
            pltpu.VMEM((blks, row_blocks, slots), jnp.int32),
            pltpu.SMEM((blks, row_blocks, slots), jnp.int32),
            pltpu.VMEM((chips, 2, rows, rows), jnp.float32),
            pltpu.VMEM((groups, 2, rows, rows), jnp.float32),
            pltpu.VMEM((2, rows, rows), jnp.float32),
            pltpu.VMEM((2, rows, rows), jnp.float32),
            dma((4,)), dma((blks,)), dma((blks,)), dma,
            dma((chips, 2, row_blocks, CUTS)), dma((chips, 2, row_blocks, CUTS)),
            dma((chips, 2, row_blocks)), dma((chips, 2, row_blocks)),
            dma((groups,)), dma((groups,)), dma((2,)), dma((2,)),
        ],
        compiler_params=pltpu.CompilerParams(
            collective_id=0, has_side_effects=True, vmem_limit_bytes=60 * 2**20
        ),
        cost_estimate=pl.CostEstimate(
            flops=2 * rows * 2 * rows * chips * slots * aux, bytes_accessed=2**20, transcendentals=0
        ),
    )(raw_blocks, metric_factor, sig_list, live_count.T)


def solution(mesh):
    placed = (P("blk", "grp", None, None), P(), P("blk", "grp"), P("blk", "grp"))
    return jax.shard_map(
        exchange_kernel, mesh=mesh, in_specs=placed, out_specs=P("blk", "grp"), check_vma=False
    )
```

time: 91.6 us -> 37.7 us (0.41)
  the two profiles are of different devices: /device:TPU:0 before, /device:TPU:7 now
where the time goes in v1:
time: 37.7 us; the launch traced here: 37.5 us
  Pallas kernels  36 us (95%)
  local copies, waits for them, and re-layouts  1.57 us (4%)
    pallas_call x1, Pallas kernels, exchange_kernel(): pl.pallas_call(functools.partial(kernel, chips, groups), out_shape=jax.Sh...  36 us
    unnamed x1, local copies, waits for them, and re-layouts  1.57 us

profile of v1, /device:TPU:7, one launch (start us, length us, event | category | flops | bytes accessed | tf_op | source)
XLA Modules:
  0.0 37.5 jit_solution(10323126867452020354)
XLA Ops:
  0.0 36.0 %shard_map.46 = f32[128,256]{1,0:T(8,128)} custom-call(bf16[2,6,64,256]{3,2,1,0:T(8,128)(2,1)} %raw_hbm.1, bf16[256,256]{1,0:T(8,128)(2,1)} %metric_hbm.1, s32[2,6]{1,0:T(2,128)} %sig_hbm.1, s32[1,2]{1,0:T(1,128)} %bitcast.1), custom_call_target="tpu_custom_call" | custom-call | flops 402653184 | bytes 1048576 | tf_op jit(solution)/shard_map/pallas_call | solution.py:391
  36.0 1.6 %copy.6 = f32[128,256]{1,0:T(8,128)} copy(f32[128,256]{1,0:T(8,128)} %shard_map.46) | data formatting | bytes 262144

commit v2 on v1

--- a/solution.py
+++ b/solution.py
@@ -19,9 +19,9 @@
 
 def kernel(
     chips, groups, raw_hbm, metric_hbm, sig_hbm, live, out,
-    raw, metric, sig_vec, sig_own, xs, own, dense, ids_vec, ids, acc, red, half_sum, swap,
+    raw, metric, sig_vec, sig_own, xs, own, dense, ids_vec, ids, acc, red, half_sum, kept_sum, swap,
     in_sem, id_send, id_recv, id_local, chain_send, chain_recv, share_send, share_recv,
-    red_send, red_recv, swap_send, swap_recv,
+    red_send, red_recv, keep_send, keep_recv, swap_send, swap_recv,
 ):
     row_blocks, slots, width, aux = raw_hbm.shape
     part = aux // 2
@@ -67,18 +67,32 @@
             device_id={"blk": to_blk, "grp": grp}, device_id_type=MESH,
         )
 
-    def red_copy(slot, to_grp):
+    share = 2 * rows // groups
+    per_core = groups // 2
+
+    def rows_of(group):
+        return pl.ds(pl.multiple_of(group * share, share), share)
+
+    def red_copy(source, slot, to_grp):
         return pltpu.make_async_remote_copy(
-            src_ref=acc.at[to_grp], dst_ref=red.at[slot],
-            send_sem=red_send.at[to_grp], recv_sem=red_recv.at[slot],
+            src_ref=acc.at[source, rows_of(to_grp)], dst_ref=red.at[source, slot],
+            send_sem=red_send.at[source, to_grp], recv_sem=red_recv.at[source, slot],
             device_id={"blk": blk, "grp": to_grp}, device_id_type=MESH,
         )
 
-    def swap_copy(to_core, slot):
+    def keep_copy(source, slot):
         return pltpu.make_async_remote_copy(
-            src_ref=half_sum.at[to_core], dst_ref=swap.at[slot],
-            send_sem=swap_send.at[to_core], recv_sem=swap_recv.at[slot],
-            device_id={"blk": grp * 2 + to_core, "grp": chip}, device_id_type=MESH,
+            src_ref=half_sum.at[source], dst_ref=kept_sum.at[rows_of(slot)],
+            send_sem=keep_send.at[source], recv_sem=keep_recv.at[slot],
+            device_id={"blk": blk, "grp": source}, device_id_type=MESH,
+        )
+
+    def swap_copy(source, from_core, slot):
+        return pltpu.make_async_remote_copy(
+            src_ref=half_sum.at[source], dst_ref=swap.at[from_core, rows_of(slot)],
+            send_sem=swap_send.at[source], recv_sem=swap_recv.at[from_core, slot],
+            device_id={"blk": source * 2 + lax.div(grp, per_core), "grp": chip},
+            device_id_type=MESH,
         )
 
     loads = [
@@ -113,10 +127,16 @@
 
     @pl.when(chip != grp)
     def _():
-        for other in range(2):
-            pl.semaphore_signal(
-                barrier, inc=1, device_id={"blk": grp * 2 + other, "grp": chip}, device_id_type=MESH
-            )
+        for slot in range(per_core):
+            group = core * per_core + slot
+
+            @pl.when(group != grp)
+            def _():
+                for other in range(2):
+                    pl.semaphore_signal(
+                        barrier, inc=1, device_id={"blk": grp * 2 + other, "grp": group},
+                        device_id_type=MESH,
+                    )
 
     for load in loads:
         load.wait()
@@ -130,12 +150,9 @@
         for half in range(2):
             piece = kept[:, half * part : (half + 1) * part]
             xs[core, chip, half, m] = piece
-            for s in range(slots):
-                own[half, m, s] = piece[s * width : (s + 1) * width]
-            own[half, m, slots] = jnp.zeros((width, part), jnp.bfloat16)
     ids_vec[blk] = sig_vec[...]
 
-    pl.semaphore_wait(barrier, 2 * chips + groups - 2 + jnp.where(chip != grp, 2, 0))
+    pl.semaphore_wait(barrier, 2 * chips + groups - 2 + jnp.where(chip != grp, chips - 1, 0))
 
     def send_ids(other, carry):
         @pl.when(other != blk)
@@ -161,13 +178,31 @@
         for m in range(row_blocks):
             share_copy(core, chip, half, m).start()
 
-    for m in range(row_blocks):
-        for n in range(NOB_DEV):
+    for half in range(2):
+        for s in range(slots):
+            block = jnp.concatenate(
+                [
+                    xs[core, chip, half, m, s * width : (s + 1) * width, :]
+                    for m in range(row_blocks)
+                ],
+                axis=0,
+            )
+            own[half, s] = block.astype(jnp.float32).T.astype(jnp.bfloat16)
+        own[half, slots] = jnp.zeros((part, rows), jnp.bfloat16)
+
+    row_block_of = lax.broadcasted_iota(jnp.int32, (part, rows), 1) // width
+    for n in range(NOB_DEV):
+        places = []
+        for m in range(row_blocks):
             at = jnp.int32(slots)
             for s in range(slots):
                 at = jnp.where(sig_own[m, s] == n, s, at)
-            for half in range(2):
-                dense[half, n, m * width : (m + 1) * width, :] = own[half, m, at]
+            places.append(at)
+        for half in range(2):
+            chosen = own[half, places[0]]
+            for m in range(1, row_blocks):
+                chosen = jnp.where(row_block_of == m, own[half, places[m]], chosen)
+            dense[half, n] = chosen
 
     acc[...] = jnp.zeros_like(acc)
 
@@ -188,17 +223,39 @@
             axis=1,
         )
         chosen = jnp.concatenate(
-            [dense[half, ids[source * 2 + from_core, m, s]] for s in range(slots)], axis=1
-        )
-        here = pl.ds(pl.multiple_of(m * width, width), width)
-        acc[source, from_core, here, :] += lax.dot_general(
-            block, chosen, (((1,), (1,)), ((), ())), preferred_element_type=jnp.float32
-        )
+            [dense[half, ids[source * 2 + from_core, m, s]] for s in range(slots)], axis=0
+        )
+        here = pl.ds(pl.multiple_of(from_core * rows + m * width, width), width)
+        acc[source, here, :] += jnp.dot(block, chosen, preferred_element_type=jnp.float32)
 
     def send_partial(source):
+        def to_group(other, carry):
+            @pl.when(other != grp)
+            def _():
+                red_copy(source, grp, other).start()
+            return carry
+
+        lax.fori_loop(0, groups, to_group, 0)
+
+    def finish(source):
+        def add_group(other, total):
+            red_copy(source, other, other).wait_recv()
+            return total + red[source, other]
+
+        total = lax.fori_loop(0, grp, add_group, acc[source, rows_of(grp), :])
+        half_sum[source] = lax.fori_loop(grp + 1, groups, add_group, total)
+
+        @pl.when(source != chip)
+        def _():
+            swap_copy(source, core, lax.rem(grp, per_core)).start()
+
         @pl.when(source != grp)
         def _():
-            red_copy(grp, source).start()
+            keep_copy(source, grp).start()
+
+        @pl.when(source == grp)
+        def _():
+            kept_sum[rows_of(grp), :] = half_sum[source]
 
     for half in range(2):
         for m in range(row_blocks):
@@ -281,36 +338,39 @@
 
     lax.fori_loop(0, (chips - 1) * row_blocks + 1, one_turn, 0)
 
+    finish(chip)
+
+    def finish_distance(step, carry):
+        for source in (chip - step, chip + step):
+            @pl.when(both(source >= 0, source <= last, contributes(chip, source)))
+            def _():
+                finish(source)
+
+        return carry
+
+    lax.fori_loop(1, chips, finish_distance, 0)
+
     mine = contributes(chip, grp)
     theirs = both(chip != grp, contributes(grp, chip))
 
     @pl.when(mine)
     def _():
+        def wait_kept(other, carry):
+            @pl.when(other != grp)
+            def _():
+                keep_copy(other, other).wait_recv()
+            return carry
+
+        lax.fori_loop(0, groups, wait_kept, 0)
         for core_at in range(2):
-            half_sum[core_at] = acc[grp, core_at]
-
-        def add_group(other, carry):
-            @pl.when(other != grp)
-            def _():
-                red_copy(other, grp).wait_recv()
-                for core_at in range(2):
-                    half_sum[core_at] += red[other, core_at]
-            return carry
-
-        lax.fori_loop(0, groups, add_group, 0)
-
-        @pl.when(chip != grp)
-        def _():
-            for core_at in range(2):
-                swap_copy(core_at, core).start()
-
-        for core_at in range(2):
-            out[:, core_at * rows : (core_at + 1) * rows] = 0.25 * half_sum[core_at].T
+            here = slice(core_at * rows, (core_at + 1) * rows)
+            out[:, here] = 0.25 * kept_sum[here, :].T
 
     @pl.when(theirs)
     def _():
         for core_at in range(2):
-            swap_copy(core_at, core_at).wait_recv()
+            for slot in range(per_core):
+                swap_copy(chip, core_at, slot).wait_recv()
 
     @pl.when(both(mine, theirs))
     def _():
@@ -365,18 +425,27 @@
                     for cut in range(CUTS):
                         chain_copy(source, half, m, cut, chip).wait_send()
 
-        @pl.when(both(source != grp, contributes(chip, source)))
-        def _():
-            red_copy(grp, source).wait_send()
+        @pl.when(contributes(chip, source))
+        def _():
+            def done_group(other, inner):
+                @pl.when(other != grp)
+                def _():
+                    red_copy(source, grp, other).wait_send()
+                return inner
+
+            lax.fori_loop(0, groups, done_group, 0)
+
+            @pl.when(source != chip)
+            def _():
+                swap_copy(source, core, 0).wait_send()
+
+            @pl.when(source != grp)
+            def _():
+                keep_copy(source, grp).wait_send()
 
         return carry
 
     lax.fori_loop(0, chips, done_source, 0)
-
-    @pl.when(both(mine, chip != grp))
-    def _():
-        for core_at in range(2):
-            swap_copy(core_at, core).wait_send()
 
 
 def exchange_kernel(raw_blocks, metric_factor, sig_list, live_count):
@@ -384,6 +453,7 @@
     blks, groups = lax.axis_size("blk"), lax.axis_size("grp")
     chips = blks // 2
     rows, part = row_blocks * width, aux // 2
+    share = 2 * rows // groups
     vmem = pl.BlockSpec(memory_space=pltpu.VMEM)
     hbm = pl.BlockSpec(memory_space=pltpu.HBM)
     smem = pl.BlockSpec(memory_space=pltpu.SMEM)
@@ -399,18 +469,20 @@
             pltpu.VMEM(sig_list.shape, jnp.int32),
             pltpu.SMEM(sig_list.shape, jnp.int32),
             pltpu.VMEM((2, chips, 2, row_blocks, slots * width, part), jnp.bfloat16),
-            pltpu.VMEM((2, row_blocks, slots + 1, width, part), jnp.bfloat16),
-            pltpu.VMEM((2, NOB_DEV, rows, part), jnp.bfloat16),
+            pltpu.VMEM((2, slots + 1, part, rows), jnp.bfloat16),
+            pltpu.VMEM((2, NOB_DEV, part, rows), jnp.bfloat16),
             pltpu.VMEM((blks, row_blocks, slots), jnp.int32),
             pltpu.SMEM((blks, row_blocks, slots), jnp.int32),
-            pltpu.VMEM((chips, 2, rows, rows), jnp.float32),
-            pltpu.VMEM((groups, 2, rows, rows), jnp.float32),
-            pltpu.VMEM((2, rows, rows), jnp.float32),
+            pltpu.VMEM((chips, 2 * rows, rows), jnp.float32),
+            pltpu.VMEM((chips, groups, share, rows), jnp.float32),
+            pltpu.VMEM((chips, share, rows), jnp.float32),
+            pltpu.VMEM((2 * rows, rows), jnp.float32),
             pltpu.VMEM((2, rows, rows), jnp.float32),
             dma((4,)), dma((blks,)), dma((blks,)), dma,
             dma((chips, 2, row_blocks, CUTS)), dma((chips, 2, row_blocks, CUTS)),
             dma((chips, 2, row_blocks)), dma((chips, 2, row_blocks)),
-            dma((groups,)), dma((groups,)), dma((2,)), dma((2,)),
+            dma((chips, groups)), dma((chips, groups)), dma((chips,)), dma((groups,)),
+            dma((chips,)), dma((2, groups // 2)),
         ],
         compiler_params=pltpu.CompilerParams(
             collective_id=0, has_side_effects=True, vmem_limit_bytes=60 * 2**20

time: 37.7 us -> 33 us (0.88)
  the two profiles are of different devices: /device:TPU:7 before, /device:TPU:6 now
where the time goes in v2:
time: 33 us; the launch traced here: 32.9 us
  Pallas kernels  31.3 us (95%)
  local copies, waits for them, and re-layouts  1.57 us (5%)
    pallas_call x1, Pallas kernels, exchange_kernel(): pl.pallas_call(functools.partial(kernel, chips, groups), out_shape=jax.Sh...  31.3 us
    unnamed x1, local copies, waits for them, and re-layouts  1.57 us

profile of v2, /device:TPU:6, one launch (start us, length us, event | category | flops | bytes accessed | tf_op | source)
XLA Modules:
  0.0 32.9 jit_solution(2719847913101119922)
XLA Ops:
  0.0 31.3 %shard_map.46 = f32[128,256]{1,0:T(8,128)} custom-call(bf16[2,6,64,256]{3,2,1,0:T(8,128)(2,1)} %raw_hbm.1, bf16[256,256]{1,0:T(8,128)(2,1)} %metric_hbm.1, s32[2,6]{1,0:T(2,128)} %sig_hbm.1, s32[1,2]{1,0:T(1,128)} %bitcast.1), custom_call_target="tpu_custom_call" | custom-call | flops 402653184 | bytes 1048576 | tf_op jit(solution)/shard_map/pallas_call | solution.py:461
  31.3 1.6 %copy.6 = f32[128,256]{1,0:T(8,128)} copy(f32[128,256]{1,0:T(8,128)} %shard_map.46) | data formatting | bytes 262144

commit v3 on v2

--- a/solution.py
+++ b/solution.py
@@ -141,6 +141,8 @@
     for load in loads:
         load.wait()
 
+    own_up = both(chip < last - 1)
+    own_down = both(chip > 1)
     slot_of_row = lax.broadcasted_iota(jnp.int32, (slots * width, aux), 0) // width
     for m in range(row_blocks):
         product = jnp.dot(
@@ -148,11 +150,21 @@
         )
         kept = jnp.where(slot_of_row < live[0, m], product, 0.0).astype(jnp.bfloat16)
         for half in range(2):
-            piece = kept[:, half * part : (half + 1) * part]
-            xs[core, chip, half, m] = piece
-    ids_vec[blk] = sig_vec[...]
-
-    pl.semaphore_wait(barrier, 2 * chips + groups - 2 + jnp.where(chip != grp, chips - 1, 0))
+            xs[core, chip, half, m] = kept[:, half * part : (half + 1) * part]
+
+        if m == 0:
+            pl.semaphore_wait(
+                barrier, 2 * chips + groups - 2 + jnp.where(chip != grp, chips - 1, 0)
+            )
+
+        for cut in range(CUTS):
+            @pl.when(own_up)
+            def _():
+                chain_copy(chip, LOW, m, cut, chip + 1).start()
+
+            @pl.when(own_down)
+            def _():
+                chain_copy(chip, HIGH, m, cut, chip - 1).start()
 
     def send_ids(other, carry):
         @pl.when(other != blk)
@@ -161,18 +173,7 @@
         return carry
 
     lax.fori_loop(0, 2 * chips, send_ids, 0)
-
-    own_up = both(chip < last - 1)
-    own_down = both(chip > 1)
-    for m in range(row_blocks):
-        for cut in range(CUTS):
-            @pl.when(own_up)
-            def _():
-                chain_copy(chip, LOW, m, cut, chip + 1).start()
-
-            @pl.when(own_down)
-            def _():
-                chain_copy(chip, HIGH, m, cut, chip - 1).start()
+    ids_vec[blk] = sig_vec[...]
 
     for half in range(2):
         for m in range(row_blocks):
@@ -206,17 +207,6 @@
 
     acc[...] = jnp.zeros_like(acc)
 
-    def wait_ids(other, carry):
-        @pl.when(other != blk)
-        def _():
-            id_copy(other, other).wait_recv()
-        return carry
-
-    lax.fori_loop(0, 2 * chips, wait_ids, 0)
-    to_scalar = pltpu.make_async_copy(ids_vec, ids, id_local)
-    to_scalar.start()
-    to_scalar.wait()
-
     def add_products(from_core, source, half, m):
         block = jnp.concatenate(
             [xs[from_core, source, half, m, s * width : (s + 1) * width, :] for s in range(slots)],
@@ -256,10 +246,6 @@
         @pl.when(source == grp)
         def _():
             kept_sum[rows_of(grp), :] = half_sum[source]
-
-    for half in range(2):
-        for m in range(row_blocks):
-            add_products(core, chip, half, m)
 
     for end, first, second, to_chip in ((0, LOW, HIGH, 1), (last, HIGH, LOW, last - 1)):
         @pl.when(chip == end)
@@ -317,6 +303,26 @@
             def _():
                 send_partial(source)
 
+    def finish_distance(step):
+        @pl.when(step == 0)
+        def _():
+            finish(chip)
+
+        below, above = chip - step, chip + step
+        from_ends = (both(step == 2, chip == 1), both(step == 2, chip == last - 1))
+        for valid, source, end, from_end in (
+            (up_valid(below), below, 0, from_ends[0]), (down_valid(above), above, last, from_ends[1])
+        ):
+            late = both(step == 1, source == end)
+
+            @pl.when(both(valid, step > 0, jnp.logical_not(late)))
+            def _():
+                finish(source)
+
+            @pl.when(from_end)
+            def _():
+                finish(end)
+
     def one_turn(turn, carry):
         @pl.when(turn < (chips - 1) * row_blocks)
         def _():
@@ -324,6 +330,19 @@
 
         @pl.when(turn == 0)
         def _():
+            @functools.partial(lax.fori_loop, 0, 2 * chips, init_val=0)
+            def _(other, carry):
+                @pl.when(other != blk)
+                def _():
+                    id_copy(other, other).wait_recv()
+                return carry
+
+            to_scalar = pltpu.make_async_copy(ids_vec, ids, id_local)
+            to_scalar.start()
+            to_scalar.wait()
+            for half in range(2):
+                for m in range(row_blocks):
+                    add_products(core, chip, half, m)
             for half in range(2):
                 for m in range(row_blocks):
                     share_copy(sibling, chip, half, m).wait_recv()
@@ -334,21 +353,14 @@
         def _():
             multiply(turn - 1)
 
+        @pl.when(both(turn > 0, lax.rem(turn, row_blocks) == 0))
+        def _():
+            finish_distance(lax.div(turn, row_blocks) - 1)
+
         return carry
 
     lax.fori_loop(0, (chips - 1) * row_blocks + 1, one_turn, 0)
-
-    finish(chip)
-
-    def finish_distance(step, carry):
-        for source in (chip - step, chip + step):
-            @pl.when(both(source >= 0, source <= last, contributes(chip, source)))
-            def _():
-                finish(source)
-
-        return carry
-
-    lax.fori_loop(1, chips, finish_distance, 0)
+    finish_distance(chips - 1)
 
     mine = contributes(chip, grp)
     theirs = both(chip != grp, contributes(grp, chip))

time: 33 us -> 36.6 us (1.11)
  Pallas kernels: 31.3 us -> 34.8 us
    pallas_call x1, Pallas kernels: 31.3 us -> 34.8 us  [exchange_kernel(): pl.pallas_call(functools.partial(kernel, chips, groups), out_shape=jax.Sh...]
where the time goes in v3:
time: 36.6 us; the launch traced here: 36.4 us
  Pallas kernels  34.8 us (95%)
  local copies, waits for them, and re-layouts  1.57 us (4%)
    pallas_call x1, Pallas kernels, exchange_kernel(): pl.pallas_call(functools.partial(kernel, chips, groups), out_shape=jax.Sh...  34.8 us
    unnamed x1, local copies, waits for them, and re-layouts  1.57 us

profile of v3, /device:TPU:6, one launch (start us, length us, event | category | flops | bytes accessed | tf_op | source)
XLA Modules:
  0.0 36.4 jit_solution(1448729327438683470)
XLA Ops:
  0.0 34.8 %shard_map.46 = f32[128,256]{1,0:T(8,128)} custom-call(bf16[2,6,64,256]{3,2,1,0:T(8,128)(2,1)} %raw_hbm.1, bf16[256,256]{1,0:T(8,128)(2,1)} %metric_hbm.1, s32[2,6]{1,0:T(2,128)} %sig_hbm.1, s32[1,2]{1,0:T(1,128)} %bitcast.1), custom_call_target="tpu_custom_call" | custom-call | flops 402653184 | bytes 1048576 | tf_op jit(solution)/shard_map/pallas_call | solution.py:473
  34.8 1.6 %copy.6 = f32[128,256]{1,0:T(8,128)} copy(f32[128,256]{1,0:T(8,128)} %shard_map.46) | data formatting | bytes 262144

commit v4 on v3

--- a/solution.py
+++ b/solution.py
@@ -141,6 +141,12 @@
     for load in loads:
         load.wait()
 
+    def send_ids(other, carry):
+        @pl.when(other != blk)
+        def _():
+            id_copy(blk, other).start()
+        return carry
+
     own_up = both(chip < last - 1)
     own_down = both(chip > 1)
     slot_of_row = lax.broadcasted_iota(jnp.int32, (slots * width, aux), 0) // width
@@ -156,6 +162,8 @@
             pl.semaphore_wait(
                 barrier, 2 * chips + groups - 2 + jnp.where(chip != grp, chips - 1, 0)
             )
+            lax.fori_loop(0, 2 * chips, send_ids, 0)
+            ids_vec[blk] = sig_vec[...]
 
         for cut in range(CUTS):
             @pl.when(own_up)
@@ -165,15 +173,6 @@
             @pl.when(own_down)
             def _():
                 chain_copy(chip, HIGH, m, cut, chip - 1).start()
-
-    def send_ids(other, carry):
-        @pl.when(other != blk)
-        def _():
-            id_copy(blk, other).start()
-        return carry
-
-    lax.fori_loop(0, 2 * chips, send_ids, 0)
-    ids_vec[blk] = sig_vec[...]
 
     for half in range(2):
         for m in range(row_blocks):
@@ -353,14 +352,14 @@
         def _():
             multiply(turn - 1)
 
-        @pl.when(both(turn > 0, lax.rem(turn, row_blocks) == 0))
-        def _():
-            finish_distance(lax.div(turn, row_blocks) - 1)
-
         return carry
 
     lax.fori_loop(0, (chips - 1) * row_blocks + 1, one_turn, 0)
-    finish_distance(chips - 1)
+
+    @functools.partial(lax.fori_loop, 0, chips, init_val=0)
+    def _(step, carry):
+        finish_distance(step)
+        return carry
 
     mine = contributes(chip, grp)
     theirs = both(chip != grp, contributes(grp, chip))
@@ -497,7 +496,7 @@
             dma((chips,)), dma((2, groups // 2)),
         ],
         compiler_params=pltpu.CompilerParams(
-            collective_id=0, has_side_effects=True, vmem_limit_bytes=60 * 2**20
+            collective_id=0, has_side_effects=True, vmem_limit_bytes=56400000
         ),
         cost_estimate=pl.CostEstimate(
             flops=2 * rows * 2 * rows * chips * slots * aux, bytes_accessed=2**20, transcendentals=0

time: 36.6 us -> 32.3 us (0.88)
  Pallas kernels: 34.8 us -> 30.6 us
    pallas_call x1, Pallas kernels: 34.8 us -> 30.6 us  [exchange_kernel(): pl.pallas_call(functools.partial(kernel, chips, groups), out_shape=jax.Sh...]
    unnamed x1 -> x5, local copies, waits for them, and re-layouts: 1.57 us -> 1.35 us
where the time goes in v4:
time: 32.3 us; the launch traced here: 31.9 us
  Pallas kernels  30.6 us (95%)
  local copies, waits for them, and re-layouts  1.35 us (4%)
    pallas_call x1, Pallas kernels, exchange_kernel(): pl.pallas_call(functools.partial(kernel, chips, groups), out_shape=jax.Sh...  30.6 us
    unnamed x5, local copies, waits for them, and re-layouts  1.35 us

profile of v4, /device:TPU:6, one launch (start us, length us, event | category | flops | bytes accessed | tf_op | source)
XLA Modules:
  0.0 31.9 jit_solution(5199618778491297758)
XLA Ops:
  0.0 0.0 copy-start.1
  0.0 0.0 copy-start
  0.0 0.7 %copy-done.1 = s32[2,1]{0,1:T(1,128)S(1)} copy-done((s32[2,1]{0,1:T(1,128)S(1)}, s32[2,1]{0,1:T(1,128)}, u32[]{:S(2)}) %copy-start.1) | copy-done | bytes 32
  0.7 0.0 copy-done
  0.7 30.6 %shard_map.46 = f32[128,256]{1,0:T(8,128)S(1)} custom-call(bf16[2,6,64,256]{3,2,1,0:T(8,128)(2,1)} %raw_hbm.1, bf16[256,256]{1,0:T(8,128)(2,1)} %metric_hbm.1, s32[2,6]{1,0:T(2,128)S(1)} %copy-done, s32[1,2]{1,0:T(1,128)S(1)} %bitcast.1), custom_call_target="tpu_custom_call" | custom-call | flops 402653184 | bytes 1048576 | tf_op jit(solution)/shard_map/pallas_call | solution.py:472
  31.3 0.7 %copy.6 = f32[128,256]{1,0:T(8,128)} copy(f32[128,256]{1,0:T(8,128)S(1)} %shard_map.46) | data formatting | bytes 262144
Async XLA Ops:
  0.0 0.7 %copy-start.1 = (s32[2,1]{0,1:T(1,128)S(1)}, s32[2,1]{0,1:T(1,128)}, u32[]{:S(2)}) copy-start(s32[2,1]{0,1:T(1,128)} %param.7) | copy-start | bytes 28
  0.0 0.7 %copy-start = (s32[2,6]{1,0:T(2,128)S(1)}, s32[2,6]{1,0:T(2,128)}, u32[]{:S(2)}) copy-start(s32[2,6]{1,0:T(2,128)} %sig_hbm.1) | copy-start | bytes 148

commit v5 on v4

--- a/solution.py
+++ b/solution.py
@@ -178,33 +178,34 @@
         for m in range(row_blocks):
             share_copy(core, chip, half, m).start()
 
-    for half in range(2):
-        for s in range(slots):
-            block = jnp.concatenate(
-                [
-                    xs[core, chip, half, m, s * width : (s + 1) * width, :]
-                    for m in range(row_blocks)
-                ],
-                axis=0,
-            )
-            own[half, s] = block.astype(jnp.float32).T.astype(jnp.bfloat16)
-        own[half, slots] = jnp.zeros((part, rows), jnp.bfloat16)
-
-    row_block_of = lax.broadcasted_iota(jnp.int32, (part, rows), 1) // width
-    for n in range(NOB_DEV):
-        places = []
-        for m in range(row_blocks):
-            at = jnp.int32(slots)
+    def lay_out():
+        for half in range(2):
             for s in range(slots):
-                at = jnp.where(sig_own[m, s] == n, s, at)
-            places.append(at)
-        for half in range(2):
-            chosen = own[half, places[0]]
-            for m in range(1, row_blocks):
-                chosen = jnp.where(row_block_of == m, own[half, places[m]], chosen)
-            dense[half, n] = chosen
-
-    acc[...] = jnp.zeros_like(acc)
+                block = jnp.concatenate(
+                    [
+                        xs[core, chip, half, m, s * width : (s + 1) * width, :]
+                        for m in range(row_blocks)
+                    ],
+                    axis=0,
+                )
+                own[half, s] = block.astype(jnp.float32).T.astype(jnp.bfloat16)
+            own[half, slots] = jnp.zeros((part, rows), jnp.bfloat16)
+
+        row_block_of = lax.broadcasted_iota(jnp.int32, (part, rows), 1) // width
+        for n in range(NOB_DEV):
+            places = []
+            for m in range(row_blocks):
+                at = jnp.int32(slots)
+                for s in range(slots):
+                    at = jnp.where(sig_own[m, s] == n, s, at)
+                places.append(at)
+            for half in range(2):
+                chosen = own[half, places[0]]
+                for m in range(1, row_blocks):
+                    chosen = jnp.where(row_block_of == m, own[half, places[m]], chosen)
+                dense[half, n] = chosen
+
+        acc[...] = jnp.zeros_like(acc)
 
     def add_products(from_core, source, half, m):
         block = jnp.concatenate(
@@ -246,24 +247,25 @@
         def _():
             kept_sum[rows_of(grp), :] = half_sum[source]
 
-    for end, first, second, to_chip in ((0, LOW, HIGH, 1), (last, HIGH, LOW, last - 1)):
-        @pl.when(chip == end)
-        def _():
-            for m in range(row_blocks):
+    def send_other_half(m):
+        for end, first, second, to_chip in ((0, LOW, HIGH, 1), (last, HIGH, LOW, last - 1)):
+            @pl.when(chip == end)
+            def _():
                 for cut in range(CUTS):
                     chain_copy(chip, first, m, cut, to_chip).wait_send()
                     chain_copy(chip, second, m, cut, to_chip).start()
 
-    def arrive(source, half, m, onward, to_chip):
-        for cut in range(CUTS):
-            chain_copy(source, half, m, cut, chip).wait_recv()
-
-            if onward is not None:
-                @pl.when(onward)
-                def _():
-                    chain_copy(source, half, m, cut, to_chip).start()
-
-        share_copy(core, source, half, m).start()
+    def arrive(source, half, m, cut, onward, to_chip):
+        chain_copy(source, half, m, cut, chip).wait_recv()
+
+        if onward is not None:
+            @pl.when(onward)
+            def _():
+                chain_copy(source, half, m, cut, to_chip).start()
+
+        @pl.when(cut == CUTS - 1)
+        def _():
+            share_copy(core, source, half, m).start()
 
     def use(source, half, m):
         add_products(core, source, half, m)
@@ -279,21 +281,27 @@
             (both(step == 2, chip == last - 1), last, LOW, None, None),
         )
 
+    def place_of(turn):
+        whole = lax.div(turn, CUTS)
+        return lax.div(whole, row_blocks) + 1, lax.rem(whole, row_blocks), lax.rem(turn, CUTS)
+
     def take_in(turn):
-        step, m = lax.div(turn, row_blocks) + 1, lax.rem(turn, row_blocks)
+        step, m, cut = place_of(turn)
         for valid, source, half, onward, to_chip in routes(step):
             @pl.when(valid)
             def _():
-                arrive(source, half, m, onward, to_chip)
+                arrive(source, half, m, cut, onward, to_chip)
 
     def multiply(turn):
-        step, m = lax.div(turn, row_blocks) + 1, lax.rem(turn, row_blocks)
+        step, m, cut = place_of(turn)
         for index, (valid, source, half, onward, to_chip) in enumerate(routes(step)):
-            @pl.when(valid)
+            now = both(valid, cut == (0, CUTS - 1)[index % 2])
+
+            @pl.when(now)
             def _():
                 use(source, half, m)
 
-            whole = both(valid, m == row_blocks - 1)
+            whole = both(now, m == row_blocks - 1)
             if index < 2:
                 from_end = both(step == 1, source == (0, last)[index])
                 whole = both(whole, jnp.logical_not(from_end))
@@ -322,12 +330,19 @@
             def _():
                 finish(end)
 
+    turns = (chips - 1) * row_blocks * CUTS
+
     def one_turn(turn, carry):
-        @pl.when(turn < (chips - 1) * row_blocks)
+        @pl.when(turn < turns)
         def _():
             take_in(turn)
 
         @pl.when(turn == 0)
+        def _():
+            lay_out()
+            send_other_half(0)
+
+        @pl.when(turn == 1)
         def _():
             @functools.partial(lax.fori_loop, 0, 2 * chips, init_val=0)
             def _(other, carry):
@@ -342,19 +357,24 @@
             for half in range(2):
                 for m in range(row_blocks):
                     add_products(core, chip, half, m)
+            for m in range(1, row_blocks):
+                send_other_half(m)
+
+        @pl.when(turn == 2)
+        def _():
             for half in range(2):
                 for m in range(row_blocks):
                     share_copy(sibling, chip, half, m).wait_recv()
                     add_products(sibling, chip, half, m)
             send_partial(chip)
 
-        @pl.when(turn > 0)
-        def _():
-            multiply(turn - 1)
-
-        return carry
-
-    lax.fori_loop(0, (chips - 1) * row_blocks + 1, one_turn, 0)
+        @pl.when(turn > 2)
+        def _():
+            multiply(turn - 3)
+
+        return carry
+
+    lax.fori_loop(0, turns + 3, one_turn, 0)
 
     @functools.partial(lax.fori_loop, 0, chips, init_val=0)
     def _(step, carry):

time: 32.3 us -> 31.6 us (0.978)
  Pallas kernels: 30.6 us -> 29.8 us
    pallas_call x1, Pallas kernels: 30.6 us -> 29.8 us  [exchange_kernel(): pl.pallas_call(functools.partial(kernel, chips, groups), out_shape=jax.Sh...]
where the time goes in v5:
time: 31.6 us; the launch traced here: 31.2 us
  Pallas kernels  29.8 us (94%)
  local copies, waits for them, and re-layouts  1.35 us (4%)
    pallas_call x1, Pallas kernels, exchange_kernel(): pl.pallas_call(functools.partial(kernel, chips, groups), out_shape=jax.Sh...  29.8 us
    unnamed x5, local copies, waits for them, and re-layouts  1.35 us

profile of v5, /device:TPU:6, one launch (start us, length us, event | category | flops | bytes accessed | tf_op | source)
XLA Modules:
  0.0 31.2 jit_solution(10593098237483652404)
XLA Ops:
  0.0 0.0 copy-start.1
  0.0 0.0 copy-start
  0.0 0.7 %copy-done.1 = s32[2,1]{0,1:T(1,128)S(1)} copy-done((s32[2,1]{0,1:T(1,128)S(1)}, s32[2,1]{0,1:T(1,128)}, u32[]{:S(2)}) %copy-start.1) | copy-done | bytes 32
  0.7 0.0 copy-done
  0.7 29.8 %shard_map.46 = f32[128,256]{1,0:T(8,128)S(1)} custom-call(bf16[2,6,64,256]{3,2,1,0:T(8,128)(2,1)} %raw_hbm.1, bf16[256,256]{1,0:T(8,128)(2,1)} %metric_hbm.1, s32[2,6]{1,0:T(2,128)S(1)} %copy-done, s32[1,2]{1,0:T(1,128)S(1)} %bitcast.1), custom_call_target="tpu_custom_call" | custom-call | flops 402653184 | bytes 1048576 | tf_op jit(solution)/shard_map/pallas_call | solution.py:492
  30.5 0.7 %copy.6 = f32[128,256]{1,0:T(8,128)} copy(f32[128,256]{1,0:T(8,128)S(1)} %shard_map.46) | data formatting | bytes 262144
Async XLA Ops:
  0.0 0.7 %copy-start.1 = (s32[2,1]{0,1:T(1,128)S(1)}, s32[2,1]{0,1:T(1,128)}, u32[]{:S(2)}) copy-start(s32[2,1]{0,1:T(1,128)} %param.7) | copy-start | bytes 28
  0.0 0.7 %copy-start = (s32[2,6]{1,0:T(2,128)S(1)}, s32[2,6]{1,0:T(2,128)}, u32[]{:S(2)}) copy-start(s32[2,6]{1,0:T(2,128)} %sig_hbm.1) | copy-start | bytes 148

commit v6 on v5

--- a/solution.py
+++ b/solution.py
@@ -9,7 +9,7 @@
 
 NOB_DEV = 16
 MESH = pl.DeviceIdType.MESH
-CUTS = 2
+CUTS = 3
 LOW, HIGH = 0, 1
 
 
@@ -178,18 +178,17 @@
         for m in range(row_blocks):
             share_copy(core, chip, half, m).start()
 
-    def lay_out():
-        for half in range(2):
-            for s in range(slots):
-                block = jnp.concatenate(
-                    [
-                        xs[core, chip, half, m, s * width : (s + 1) * width, :]
-                        for m in range(row_blocks)
-                    ],
-                    axis=0,
-                )
-                own[half, s] = block.astype(jnp.float32).T.astype(jnp.bfloat16)
-            own[half, slots] = jnp.zeros((part, rows), jnp.bfloat16)
+    def lay_out(half):
+        for s in range(slots):
+            block = jnp.concatenate(
+                [
+                    xs[core, chip, half, m, s * width : (s + 1) * width, :]
+                    for m in range(row_blocks)
+                ],
+                axis=0,
+            )
+            own[half, s] = block.astype(jnp.float32).T.astype(jnp.bfloat16)
+        own[half, slots] = jnp.zeros((part, rows), jnp.bfloat16)
 
         row_block_of = lax.broadcasted_iota(jnp.int32, (part, rows), 1) // width
         for n in range(NOB_DEV):
@@ -199,13 +198,11 @@
                 for s in range(slots):
                     at = jnp.where(sig_own[m, s] == n, s, at)
                 places.append(at)
-            for half in range(2):
-                chosen = own[half, places[0]]
-                for m in range(1, row_blocks):
-                    chosen = jnp.where(row_block_of == m, own[half, places[m]], chosen)
-                dense[half, n] = chosen
-
-        acc[...] = jnp.zeros_like(acc)
+            chosen = own[half, places[0]]
+            for m in range(1, row_blocks):
+                chosen = jnp.where(row_block_of == m, own[half, places[m]], chosen)
+            dense[half, n] = chosen
+
 
     def add_products(from_core, source, half, m):
         block = jnp.concatenate(
@@ -339,10 +336,15 @@
 
         @pl.when(turn == 0)
         def _():
-            lay_out()
+            lay_out(LOW)
+            acc[...] = jnp.zeros_like(acc)
+
+        @pl.when(turn == 1)
+        def _():
+            lay_out(HIGH)
             send_other_half(0)
 
-        @pl.when(turn == 1)
+        @pl.when(turn == 2)
         def _():
             @functools.partial(lax.fori_loop, 0, 2 * chips, init_val=0)
             def _(other, carry):
@@ -360,7 +362,7 @@
             for m in range(1, row_blocks):
                 send_other_half(m)
 
-        @pl.when(turn == 2)
+        @pl.when(turn == 3)
         def _():
             for half in range(2):
                 for m in range(row_blocks):
@@ -368,13 +370,13 @@
                     add_products(sibling, chip, half, m)
             send_partial(chip)
 
-        @pl.when(turn > 2)
-        def _():
-            multiply(turn - 3)
-
-        return carry
-
-    lax.fori_loop(0, turns + 3, one_turn, 0)
+        @pl.when(turn > 3)
+        def _():
+            multiply(turn - 4)
+
+        return carry
+
+    lax.fori_loop(0, turns + 4, one_turn, 0)
 
     @functools.partial(lax.fori_loop, 0, chips, init_val=0)
     def _(step, carry):

time: 31.6 us -> 32.4 us (1.025)
  Pallas kernels: 29.8 us -> 30.6 us
    pallas_call x1, Pallas kernels: 29.8 us -> 30.6 us  [exchange_kernel(): pl.pallas_call(functools.partial(kernel, chips, groups), out_shape=jax.Sh...]
where the time goes in v6:
time: 32.4 us; the launch traced here: 32 us
  Pallas kernels  30.6 us (94%)
  local copies, waits for them, and re-layouts  1.35 us (4%)
    pallas_call x1, Pallas kernels, exchange_kernel(): pl.pallas_call(functools.partial(kernel, chips, groups), out_shape=jax.Sh...  30.6 us
    unnamed x5, local copies, waits for them, and re-layouts  1.35 us

profile of v6, /device:TPU:6, one launch (start us, length us, event | category | flops | bytes accessed | tf_op | source)
XLA Modules:
  0.0 32.0 jit_solution(7381164256562554988)
XLA Ops:
  0.0 0.0 copy-start.1
  0.0 0.0 copy-start
  0.0 0.7 %copy-done.1 = s32[2,1]{0,1:T(1,128)S(1)} copy-done((s32[2,1]{0,1:T(1,128)S(1)}, s32[2,1]{0,1:T(1,128)}, u32[]{:S(2)}) %copy-start.1) | copy-done | bytes 32
  0.7 0.0 copy-done
  0.7 30.6 %shard_map.46 = f32[128,256]{1,0:T(8,128)S(1)} custom-call(bf16[2,6,64,256]{3,2,1,0:T(8,128)(2,1)} %raw_hbm.1, bf16[256,256]{1,0:T(8,128)(2,1)} %metric_hbm.1, s32[2,6]{1,0:T(2,128)S(1)} %copy-done, s32[1,2]{1,0:T(1,128)S(1)} %bitcast.1), custom_call_target="tpu_custom_call" | custom-call | flops 402653184 | bytes 1048576 | tf_op jit(solution)/shard_map/pallas_call | solution.py:494
  31.3 0.7 %copy.6 = f32[128,256]{1,0:T(8,128)} copy(f32[128,256]{1,0:T(8,128)S(1)} %shard_map.46) | data formatting | bytes 262144
Async XLA Ops:
  0.0 0.7 %copy-start.1 = (s32[2,1]{0,1:T(1,128)S(1)}, s32[2,1]{0,1:T(1,128)}, u32[]{:S(2)}) copy-start(s32[2,1]{0,1:T(1,128)} %param.7) | copy-start | bytes 28
  0.0 0.7 %copy-start = (s32[2,6]{1,0:T(2,128)S(1)}, s32[2,6]{1,0:T(2,128)}, u32[]{:S(2)}) copy-start(s32[2,6]{1,0:T(2,128)} %sig_hbm.1) | copy-start | bytes 148

commit v7 on v5

--- a/solution.py
+++ b/solution.py
@@ -218,14 +218,16 @@
         here = pl.ds(pl.multiple_of(from_core * rows + m * width, width), width)
         acc[source, here, :] += jnp.dot(block, chosen, preferred_element_type=jnp.float32)
 
-    def send_partial(source):
-        def to_group(other, carry):
-            @pl.when(other != grp)
-            def _():
-                red_copy(source, grp, other).start()
-            return carry
-
-        lax.fori_loop(0, groups, to_group, 0)
+    per_block = per_core // row_blocks
+
+    def send_partial(source, m):
+        for core_at in range(2):
+            for place in range(per_block):
+                other = core_at * per_core + m * per_block + place
+
+                @pl.when(other != grp)
+                def _():
+                    red_copy(source, grp, other).start()
 
     def finish(source):
         def add_group(other, total):
@@ -301,14 +303,14 @@
             def _():
                 use(source, half, m)
 
-            whole = both(now, m == row_blocks - 1)
+            whole = now
             if index < 2:
                 from_end = both(step == 1, source == (0, last)[index])
                 whole = both(whole, jnp.logical_not(from_end))
 
             @pl.when(whole)
             def _():
-                send_partial(source)
+                send_partial(source, m)
 
     def finish_distance(step):
         @pl.when(step == 0)
@@ -366,7 +368,8 @@
                 for m in range(row_blocks):
                     share_copy(sibling, chip, half, m).wait_recv()
                     add_products(sibling, chip, half, m)
-            send_partial(chip)
+            for m in range(row_blocks):
+                send_partial(chip, m)
 
         @pl.when(turn > 2)
         def _():
@@ -380,38 +383,6 @@
     def _(step, carry):
         finish_distance(step)
         return carry
-
-    mine = contributes(chip, grp)
-    theirs = both(chip != grp, contributes(grp, chip))
-
-    @pl.when(mine)
-    def _():
-        def wait_kept(other, carry):
-            @pl.when(other != grp)
-            def _():
-                keep_copy(other, other).wait_recv()
-            return carry
-
-        lax.fori_loop(0, groups, wait_kept, 0)
-        for core_at in range(2):
-            here = slice(core_at * rows, (core_at + 1) * rows)
-            out[:, here] = 0.25 * kept_sum[here, :].T
-
-    @pl.when(theirs)
-    def _():
-        for core_at in range(2):
-            for slot in range(per_core):
-                swap_copy(chip, core_at, slot).wait_recv()
-
-    @pl.when(both(mine, theirs))
-    def _():
-        for core_at in range(2):
-            out[:, core_at * rows : (core_at + 1) * rows] += 0.25 * swap[core_at]
-
-    @pl.when(jnp.logical_not(mine))
-    def _():
-        for core_at in range(2):
-            out[:, core_at * rows : (core_at + 1) * rows] = 0.25 * swap[core_at]
 
     def done_ids(other, carry):
         @pl.when(other != blk)
@@ -466,6 +437,45 @@
 
             lax.fori_loop(0, groups, done_group, 0)
 
+        return carry
+
+    lax.fori_loop(0, chips, done_source, 0)
+
+    mine = contributes(chip, grp)
+    theirs = both(chip != grp, contributes(grp, chip))
+
+    @pl.when(mine)
+    def _():
+        def wait_kept(other, carry):
+            @pl.when(other != grp)
+            def _():
+                keep_copy(other, other).wait_recv()
+            return carry
+
+        lax.fori_loop(0, groups, wait_kept, 0)
+        for core_at in range(2):
+            here = slice(core_at * rows, (core_at + 1) * rows)
+            out[:, here] = 0.25 * kept_sum[here, :].T
+
+    @pl.when(theirs)
+    def _():
+        for core_at in range(2):
+            for slot in range(per_core):
+                swap_copy(chip, core_at, slot).wait_recv()
+
+    @pl.when(both(mine, theirs))
+    def _():
+        for core_at in range(2):
+            out[:, core_at * rows : (core_at + 1) * rows] += 0.25 * swap[core_at]
+
+    @pl.when(jnp.logical_not(mine))
+    def _():
+        for core_at in range(2):
+            out[:, core_at * rows : (core_at + 1) * rows] = 0.25 * swap[core_at]
+
+    def done_sums(source, carry):
+        @pl.when(contributes(chip, source))
+        def _():
             @pl.when(source != chip)
             def _():
                 swap_copy(source, core, 0).wait_send()
@@ -476,7 +486,7 @@
 
         return carry
 
-    lax.fori_loop(0, chips, done_source, 0)
+    lax.fori_loop(0, chips, done_sums, 0)
 
 
 def exchange_kernel(raw_blocks, metric_factor, sig_list, live_count):

time: 31.6 us -> 30.3 us (0.959)
  Pallas kernels: 29.8 us -> 28.5 us
    pallas_call x1, Pallas kernels: 29.8 us -> 28.5 us  [exchange_kernel(): pl.pallas_call(functools.partial(kernel, chips, groups), out_shape=jax.Sh...]
where the time goes in v7:
time: 30.3 us; the launch traced here: 29.9 us
  Pallas kernels  28.5 us (94%)
  local copies, waits for them, and re-layouts  1.35 us (4%)
    pallas_call x1, Pallas kernels, exchange_kernel(): pl.pallas_call(functools.partial(kernel, chips, groups), out_shape=jax.Sh...  28.5 us
    unnamed x5, local copies, waits for them, and re-layouts  1.35 us

profile of v7, /device:TPU:6, one launch (start us, length us, event | category | flops | bytes accessed | tf_op | source)
XLA Modules:
  0.0 29.9 jit_solution(15646461762251068967)
XLA Ops:
  0.0 0.0 copy-start.1
  0.0 0.0 copy-start
  0.0 0.7 %copy-done.1 = s32[2,1]{0,1:T(1,128)S(1)} copy-done((s32[2,1]{0,1:T(1,128)S(1)}, s32[2,1]{0,1:T(1,128)}, u32[]{:S(2)}) %copy-start.1) | copy-done | bytes 32
  0.7 0.0 copy-done
  0.7 28.5 %shard_map.46 = f32[128,256]{1,0:T(8,128)S(1)} custom-call(bf16[2,6,64,256]{3,2,1,0:T(8,128)(2,1)} %raw_hbm.1, bf16[256,256]{1,0:T(8,128)(2,1)} %metric_hbm.1, s32[2,6]{1,0:T(2,128)S(1)} %copy-done, s32[1,2]{1,0:T(1,128)S(1)} %bitcast.1), custom_call_target="tpu_custom_call" | custom-call | flops 402653184 | bytes 1048576 | tf_op jit(solution)/shard_map/pallas_call | solution.py:502
  29.2 0.7 %copy.6 = f32[128,256]{1,0:T(8,128)} copy(f32[128,256]{1,0:T(8,128)S(1)} %shard_map.46) | data formatting | bytes 262144
Async XLA Ops:
  0.0 0.7 %copy-start.1 = (s32[2,1]{0,1:T(1,128)S(1)}, s32[2,1]{0,1:T(1,128)}, u32[]{:S(2)}) copy-start(s32[2,1]{0,1:T(1,128)} %param.7) | copy-start | bytes 28
  0.0 0.7 %copy-start = (s32[2,6]{1,0:T(2,128)S(1)}, s32[2,6]{1,0:T(2,128)}, u32[]{:S(2)}) copy-start(s32[2,6]{1,0:T(2,128)} %sig_hbm.1) | copy-start | bytes 148

commit v8 on v7

--- a/solution.py
+++ b/solution.py
@@ -178,18 +178,17 @@
         for m in range(row_blocks):
             share_copy(core, chip, half, m).start()
 
-    def lay_out():
-        for half in range(2):
-            for s in range(slots):
-                block = jnp.concatenate(
-                    [
-                        xs[core, chip, half, m, s * width : (s + 1) * width, :]
-                        for m in range(row_blocks)
-                    ],
-                    axis=0,
-                )
-                own[half, s] = block.astype(jnp.float32).T.astype(jnp.bfloat16)
-            own[half, slots] = jnp.zeros((part, rows), jnp.bfloat16)
+    def lay_out(half):
+        for s in range(slots):
+            block = jnp.concatenate(
+                [
+                    xs[core, chip, half, m, s * width : (s + 1) * width, :]
+                    for m in range(row_blocks)
+                ],
+                axis=0,
+            )
+            own[half, s] = block.astype(jnp.float32).T.astype(jnp.bfloat16)
+        own[half, slots] = jnp.zeros((part, rows), jnp.bfloat16)
 
         row_block_of = lax.broadcasted_iota(jnp.int32, (part, rows), 1) // width
         for n in range(NOB_DEV):
@@ -199,13 +198,10 @@
                 for s in range(slots):
                     at = jnp.where(sig_own[m, s] == n, s, at)
                 places.append(at)
-            for half in range(2):
-                chosen = own[half, places[0]]
-                for m in range(1, row_blocks):
-                    chosen = jnp.where(row_block_of == m, own[half, places[m]], chosen)
-                dense[half, n] = chosen
-
-        acc[...] = jnp.zeros_like(acc)
+            chosen = own[half, places[0]]
+            for m in range(1, row_blocks):
+                chosen = jnp.where(row_block_of == m, own[half, places[m]], chosen)
+            dense[half, n] = chosen
 
     def add_products(from_core, source, half, m):
         block = jnp.concatenate(
@@ -341,11 +337,14 @@
 
         @pl.when(turn == 0)
         def _():
-            lay_out()
+            lay_out(LOW)
+            acc[...] = jnp.zeros_like(acc)
+
+        @pl.when(turn == 1)
+        def _():
+            lay_out(HIGH)
             send_other_half(0)
 
-        @pl.when(turn == 1)
-        def _():
             @functools.partial(lax.fori_loop, 0, 2 * chips, init_val=0)
             def _(other, carry):
                 @pl.when(other != blk)
@@ -356,14 +355,15 @@
             to_scalar = pltpu.make_async_copy(ids_vec, ids, id_local)
             to_scalar.start()
             to_scalar.wait()
-            for half in range(2):
-                for m in range(row_blocks):
-                    add_products(core, chip, half, m)
+            for m in range(row_blocks):
+                add_products(core, chip, LOW, m)
+
+        @pl.when(turn == 2)
+        def _():
             for m in range(1, row_blocks):
                 send_other_half(m)
-
-        @pl.when(turn == 2)
-        def _():
+            for m in range(row_blocks):
+                add_products(core, chip, HIGH, m)
             for half in range(2):
                 for m in range(row_blocks):
                     share_copy(sibling, chip, half, m).wait_recv()

time: 30.3 us -> 30.7 us (1.013)
  Pallas kernels: 28.5 us -> 29.2 us
    pallas_call x1, Pallas kernels: 28.5 us -> 29.2 us  [exchange_kernel(): pl.pallas_call(functools.partial(kernel, chips, groups), out_shape=jax.Sh...]
where the time goes in v8:
time: 30.7 us; the launch traced here: 30.5 us
  Pallas kernels  29.2 us (95%)
  local copies, waits for them, and re-layouts  1.35 us (4%)
    pallas_call x1, Pallas kernels, exchange_kernel(): pl.pallas_call(functools.partial(kernel, chips, groups), out_shape=jax.Sh...  29.2 us
    unnamed x5, local copies, waits for them, and re-layouts  1.35 us

profile of v8, /device:TPU:6, one launch (start us, length us, event | category | flops | bytes accessed | tf_op | source)
XLA Modules:
  0.0 30.5 jit_solution(7121421614918739161)
XLA Ops:
  0.0 0.0 copy-start.1
  0.0 0.0 copy-start
  0.0 0.7 %copy-done.1 = s32[2,1]{0,1:T(1,128)S(1)} copy-done((s32[2,1]{0,1:T(1,128)S(1)}, s32[2,1]{0,1:T(1,128)}, u32[]{:S(2)}) %copy-start.1) | copy-done | bytes 32
  0.7 0.0 copy-done
  0.7 29.2 %shard_map.46 = f32[128,256]{1,0:T(8,128)S(1)} custom-call(bf16[2,6,64,256]{3,2,1,0:T(8,128)(2,1)} %raw_hbm.1, bf16[256,256]{1,0:T(8,128)(2,1)} %metric_hbm.1, s32[2,6]{1,0:T(2,128)S(1)} %copy-done, s32[1,2]{1,0:T(1,128)S(1)} %bitcast.1), custom_call_target="tpu_custom_call" | custom-call | flops 402653184 | bytes 1048576 | tf_op jit(solution)/shard_map/pallas_call | solution.py:502
  29.9 0.7 %copy.6 = f32[128,256]{1,0:T(8,128)} copy(f32[128,256]{1,0:T(8,128)S(1)} %shard_map.46) | data formatting | bytes 262144
Async XLA Ops:
  0.0 0.7 %copy-start.1 = (s32[2,1]{0,1:T(1,128)S(1)}, s32[2,1]{0,1:T(1,128)}, u32[]{:S(2)}) copy-start(s32[2,1]{0,1:T(1,128)} %param.7) | copy-start | bytes 28
  0.0 0.7 %copy-start = (s32[2,6]{1,0:T(2,128)S(1)}, s32[2,6]{1,0:T(2,128)}, u32[]{:S(2)}) copy-start(s32[2,6]{1,0:T(2,128)} %sig_hbm.1) | copy-start | bytes 148
